TPU v7x, 32 devices: a whole 2x2x4 slice. The times are simulated.
32 devices in a mesh: groups: 2 (over y), rows: 4 (over z), tm: 2 (over x), dp: 2 (over core).
Axes of the slice: x: 2, y: 2, z: 4, core: 2. Of those that a mesh axis runs over, the one named last changes fastest.
Arguments:
- frames_in: bfloat16 [4, 4, 16, 320, 128], P(('groups', 'dp'), 'tm', 'rows'), parts along dimension 0, may hold values from -6 to 6
- gain: float32 [128], replicated, may hold values from 0.5 to 1.5
- spatial_w: bfloat16 [3, 3, 128, 128], replicated, may hold values from -0.1875 to 0.1875
- temporal_w: bfloat16 [3, 128, 128], replicated, may hold values from -0.3125 to 0.3125
- cotangent: bfloat16 [4, 4, 16, 320, 128], P(('groups', 'dp'), 'tm', 'rows'), parts along dimension 0, may hold values from -6 to 6
Outputs:
- block_out: bfloat16 [4, 4, 16, 320, 128], P(('groups', 'dp'), 'tm', 'rows'), parts along dimension 0
- grad_input: bfloat16 [4, 4, 16, 320, 128], P(('groups', 'dp'), 'tm', 'rows'), parts along dimension 0
- grad_spatial: float32 [6, 3, 128, 128], P('groups'), parts along dimension 0
- grad_temporal: float32 [6, 128, 128], P('groups'), parts along dimension 0
- grad_gain: float32 [256], P('groups'), parts along dimension 0
There are 2 independent parts, one for each index of `groups`. A program takes and returns all parts, laid end to end along the dimension named above; an argument that names none is the same for every part. Nothing has to cross between parts.
All inputs are finite; a program needn't handle non-finite values.
Results may differ from a plain program's by a relative error of at most 0.0054.
Values may be sent and summed in bfloat16 or wider, within the bound.
A program may use at most 64 MiB of HBM per device.

v0:
```python
import math

import jax
import jax.numpy as jnp
from jax import lax
from jax.sharding import PartitionSpec as P

EPS = 1e-06


def extended(shard, sides, width):
    for axis, dim in sides:
        size, length = (lax.axis_size(axis), shard.shape[dim])
        up = [(i, (i + 1) % size) for i in range(size - 1)]
        down = [(j, i) for i, j in up]
        last = lax.slice_in_dim(shard, length - width, length, axis=dim)
        first = lax.slice_in_dim(shard, 0, width, axis=dim)
        before = lax.ppermute(last, axis, up)
        after = lax.ppermute(first, axis, down)
        shard = jnp.concatenate([before, shard, after], axis=dim)
    return shard


def passed_along(shard, axis, by):
    length = lax.axis_size(axis)
    pairs = [(i, i + by) for i in range(length) if 0 <= i + by < length]
    return lax.ppermute(shard, axis, pairs)


def flatten(block):
    return block.reshape(-1, block.shape[-1])


def product(left, right):
    return jnp.dot(flatten(left), right, preferred_element_type=jnp.float32)


def outer_sum(left, right):
    return lax.dot_general(
        flatten(left), flatten(right), (((0,), (0,)), ((), ())), preferred_element_type=jnp.float32
    )


def spatial_back(padded, kernel, height, width):
    total = None
    for i in range(3):
        for j in range(3):
            term = product(
                padded[:, :, 2 - i : 2 - i + height, 2 - j : 2 - j + width], kernel[i, j].T
            )
            total = term if total is None else total + term
    return total


def shards(frames_in, gain, spatial_w, temporal_w, cotangent):
    clips, frames, height, width, chans = frames_in.shape
    lead = (clips, frames, height, width, chans)
    upper = frames_in.astype(jnp.float32)
    recip = lax.rsqrt(jnp.mean(upper * upper, axis=-1, keepdims=True) + EPS)
    unit = upper * recip
    normed = (unit * gain).astype(jnp.bfloat16)
    banded = extended(normed, (("rows", 2),), 1)
    padded = jnp.pad(banded, ((0, 0), (0, 0), (0, 0), (1, 1), (0, 0)))
    hidden = None
    for i in range(3):
        for j in range(3):
            term = product(padded[:, :, i : i + height, j : j + width], spatial_w[i, j])
            hidden = term if hidden is None else hidden + term
    hidden = hidden.reshape(lead)
    act = jax.nn.silu(hidden).astype(jnp.bfloat16)
    earlier = passed_along(act, "tm", 1)
    act_pad = jnp.concatenate([earlier, act], axis=1)
    mixed = product(act_pad[:, 2 : 2 + frames], temporal_w[0])
    for k in range(1, 3):
        mixed = mixed + product(act_pad[:, 2 - k : 2 - k + frames], temporal_w[k])
    block_out = (upper + mixed.reshape(lead)).astype(jnp.bfloat16)
    later = passed_along(cotangent, "tm", -1)
    cot_pad = jnp.concatenate([cotangent, later], axis=1)
    dact = product(cot_pad[:, 0:frames], temporal_w[0].T)
    for k in range(1, 3):
        dact = dact + product(cot_pad[:, k : k + frames], temporal_w[k].T)
    sig = jax.nn.sigmoid(hidden)
    dhid = (dact.reshape(lead) * sig * (1.0 + hidden * (1.0 - sig))).astype(jnp.bfloat16)
    grad_temporal = jnp.stack(
        [outer_sum(act_pad[:, 2 - k : 2 - k + frames], cotangent) for k in range(3)]
    )
    cells_all = (
        clips
        * frames
        * height
        * width
        * lax.axis_size("rows")
        * lax.axis_size("tm")
        * lax.axis_size("dp")
    )
    scale = 1.0 / math.sqrt(cells_all)
    dzero = jnp.pad(dhid, ((0, 0), (0, 0), (2, 2), (1, 1), (0, 0)))
    whole = spatial_back(dzero, spatial_w, height + 2, width).reshape(
        (clips, frames, height + 2, width, chans)
    )
    from_above = passed_along(whole[:, :, height + 1 :].astype(jnp.bfloat16), "rows", 1).astype(
        jnp.float32
    )
    from_below = passed_along(whole[:, :, 0:1].astype(jnp.bfloat16), "rows", -1).astype(jnp.float32)
    dnorm = whole[:, :, 1 : height + 1]
    dnorm = dnorm.at[:, :, 0:1].add(from_above)
    dnorm = dnorm.at[:, :, height - 1 : height].add(from_below)
    spatial_rows = []
    for i in range(3):
        spatial_cols = []
        for j in range(3):
            spatial_cols.append(outer_sum(padded[:, :, i : i + height, j : j + width], dhid))
        spatial_rows.append(jnp.stack(spatial_cols))
    grad_spatial = jnp.stack(spatial_rows)
    grad_gain = jnp.sum(dnorm * unit, axis=(0, 1, 2, 3))
    grad_spatial, grad_temporal, grad_gain = lax.psum(
        (grad_spatial, grad_temporal, grad_gain), ("rows", "tm", "dp")
    )
    dunit = dnorm * gain
    grad_input = (
        cotangent.astype(jnp.float32)
        + recip * (dunit - unit * jnp.mean(dunit * unit, axis=-1, keepdims=True))
    ).astype(jnp.bfloat16)
    return (block_out, grad_input, grad_spatial * scale, grad_temporal * scale, grad_gain * scale)


def solution(mesh):
    return jax.shard_map(
        shards,
        mesh=mesh,
        in_specs=(
            P(("groups", "dp"), "tm", "rows", None, None),
            P(),
            P(),
            P(),
            P(("groups", "dp"), "tm", "rows", None, None),
        ),
        out_specs=(
            P(("groups", "dp"), "tm", "rows", None, None),
            P(("groups", "dp"), "tm", "rows", None, None),
            P("groups", None, None, None),
            P("groups", None, None),
            P("groups"),
        ),
        check_vma=False,
    )
```

profile of v0, /device:TPU:0, one launch (start us, length us, event | category | flops | bytes accessed | tf_op | source)
XLA Modules:
  0.0 192.7 jit_solution(13148399722400150449)
XLA Ops:
  7.2 1.6 fusion.13
  8.9 1.5 fusion.6
  10.4 4.9 %collective-permute-start = (bf16[1,2,1,320,128]{4,3,2,1,0:T(8,128)(2,1)S(1)}, bf16[1,2,1,320,128]{4,3,2,1,0:T(8,128)(2,1)S(1)}, u32[]{:S(2)}, u32[]{:S(2)}) collective-permute-start(bf16[1,2,1,320,128]{4,3,2,1,0:T(8,128)(2,1)S(1)} %get-tuple-element.58), channel_id=1, source_target_pairs={{0,4},{4,8},{8,12},{1,5},{5,9},{9,13},{2,6},{6,10},{10,14},{3,7},{... | collective-permute-start | bytes 491528 | tf_op jit(solution)/shard_map/ppermute | solution.py:18
  15.4 1.3 collective-permute-start.1
  16.7 1.3 collective-permute-start.3
  18.8 4.1 %collective-permute-done.1 = bf16[1,2,1,320,128]{4,3,2,1,0:T(8,128)(2,1)S(1)} collective-permute-done((bf16[1,2,1,320,128]{4,3,2,1,0:T(8,128)(2,1)S(1)}, bf16[1,2,1,320,128]{4,3,2,1,0:T(8,128)(2,1)S(1)}, u32[]{:S(2)}, u32[]{:S(2)}) %collective-permute-start.1) | collective-permute-done | bytes 163872 | tf_op jit(solution)/shard_map/ppermute | solution.py:19
  23.2 0.8 fusion.95
  26.8 7.9 %collective-permute-done.3 = bf16[1,2,4,320,128]{4,3,2,1,0:T(8,128)(2,1)S(1)} collective-permute-done((bf16[1,2,4,320,128]{4,3,2,1,0:T(8,128)(2,1)S(1)}, bf16[1,2,4,320,128]{4,3,2,1,0:T(8,128)(2,1)S(1)}, u32[]{:S(2)}, u32[]{:S(2)}) %collective-permute-start.3) | collective-permute-done | bytes 655392 | tf_op jit(solution)/shard_map/ppermute | solution.py:27
  35.5 0.8 multiply_convert_fusion
  39.8 1.5 multiply_convert_fusion.1
  41.3 2.1 %pad_slice_fusion = (bf16[1,2,6,320,128]{4,3,2,1,0:T(8,128)(2,1)S(1)}, bf16[1,2,6,320,128]{4,3,2,1,0:T(8,128)(2,1)S(1)}, bf16[1,2,6,320,128]{4,3,2,1,0:T(8,128)(...) fusion(bf16[1,2,4,320,128]{4,3,2,1,0:T(8,128)(2,1)S(1)} %get-tu, ...), kind=kLoop, calls=%fused_computation.22 | loop fusion | bytes 9502720 | tf_op jit(solution)/shard_map/slice | solution.py:49
  47.4 1.5 collective-permute-start.2
  48.9 1.4 fusion.42
  50.3 1.3 collective-permute-start.5
  51.6 4.9 %collective-permute-start.4 = (bf16[1,2,1,320,128]{4,3,2,1,0:T(8,128)(2,1)S(1)}, bf16[1,2,1,320,128]{4,3,2,1,0:T(8,128)(2,1)S(1)}, u32[]{:S(2)}, u32[]{:S(2)}) collective-permute-start(bf16[1,2,1,320,128]{4,3,2,1,0:T(8,128)(2,1)S(1)} %get-tuple-element.44), channel_id=1, source_target_pairs={{0,4},{4,8},{8,12},{1,5},{5,9},{9,13},{2,6},{6,10},{10,14},{3,7},{... | collective-permute-start | bytes 491528 | tf_op jit(solution)/shard_map/ppermute | solution.py:27
  56.6 0.9 pad_maximum_fusion.4
  57.8 1.5 collective-permute-done.4
  59.5 0.9 fusion.12
  60.4 30.0 %psum.23 = f32[128]{0:T(128)S(1)} all-reduce(f32[128]{0:T(128)S(1)} %get-tuple-element.29), channel_id=1, replica_groups=mesh['groups'=2,'rows'=4,'tm'=2,'dp'=2] {'rows','tm','dp'}, use_global_device_ids=true, to_apply=%region_5.6 | all-reduce | flops 128 | bytes 1024 | tf_op jit(solution)/shard_map/psum | solution.py:116
  90.9 1.0 pad_maximum_fusion.1
  93.5 1.8 convolution_add_fusion.11
  95.7 1.6 fusion.11
  97.3 85.9 %all-reduce.5.cloned.1.call-done = (f32[3,3,128,128]{3,2,1,0:T(8,128)}, f32[3,128,128]{2,1,0:T(8,128)}) async-done(((f32[3,3,128,128]{3,2,1,0:T(8,128)}, f32[3,128,128]{2,1,0:T(8,128)}), (f32[3,3,128,128]{3,2,1,0:T(8,128)}, f32[3,128,128]{2,1,0:T(8,128)})) %all-reduce.5.cloned.1.call-update) | async-done | bytes 786448 | tf_op jit(solution)/shard_map/psum | solution.py:116
  183.2 2.0 %broadcast_multiply_fusion = f32[3,3,128,128]{3,2,1,0:T(8,128)} fusion(f32[3,3,128,128]{3,2,1,0:T(8,128)} %get-tuple-element.31), kind=kLoop, calls=%fused_computation.94 | loop fusion | flops 147456 | bytes 1179648 | tf_op jit(solution)/shard_map/mul | solution.py:124
  (68 shorter events, 15.6 us)
Async XLA Ops:
  7.2 9.5 %copy-start = (bf16[1,2,4,320,128]{4,3,2,1,0:T(8,128)(2,1)S(1)}, bf16[1,2,4,320,128]{4,3,2,1,0:T(8,128)(2,1)}, u32[]{:S(2)}) copy-start(bf16[1,2,4,320,128]{4,3,2,1,0:T(8,128)(2,1)} %param.13) | copy-start | bytes 1966084
  7.2 10.8 %copy-start.4 = (bf16[3,128,128]{2,1,0:T(8,128)(2,1)S(1)}, bf16[3,128,128]{2,1,0:T(8,128)(2,1)}, u32[]{:S(2)}) copy-start(bf16[3,128,128]{2,1,0:T(8,128)(2,1)} %param.12) | copy-start | bytes 294916
  7.2 176.0 %all-reduce.5.cloned.1.call-start = ((), (), s32[]{:S(2)}) async-start(), calls=%async_computation | async-start | bytes 1572864 | tf_op jit(solution)/shard_map/psum | solution.py:116
  10.4 8.4 %collective-permute-start = (bf16[1,2,1,320,128]{4,3,2,1,0:T(8,128)(2,1)S(1)}, bf16[1,2,1,320,128]{4,3,2,1,0:T(8,128)(2,1)S(1)}, u32[]{:S(2)}, u32[]{:S(2)}) collective-permute-start(bf16[1,2,1,320,128]{4,3,2,1,0:T(8,128)(2,1)S(1)} %get-tuple-element.58), channel_id=1, source_target_pairs={{0,4},{4,8},{8,12},{1,5},{5,9},{9,13},{2,6},{6,10},{10,14},{3,7},{... | collective-permute-start | bytes 491528 | tf_op jit(solution)/shard_map/ppermute | solution.py:18
  15.4 7.6 %collective-permute-start.1 = (bf16[1,2,1,320,128]{4,3,2,1,0:T(8,128)(2,1)S(1)}, bf16[1,2,1,320,128]{4,3,2,1,0:T(8,128)(2,1)S(1)}, u32[]{:S(2)}, u32[]{:S(2)}) collective-permute-start(bf16[1,2,1,320,128]{4,3,2,1,0:T(8,128)(2,1)S(1)} %get-tuple-element.59), channel_id=1, source_target_pairs={{4,0},{8,4},{12,8},{5,1},{9,5},{13,9},{6,2},{10,6},{14,10},{7,3},{... | collective-permute-start | bytes 491528 | tf_op jit(solution)/shard_map/ppermute | solution.py:19
  16.7 18.1 %collective-permute-start.3 = (bf16[1,2,4,320,128]{4,3,2,1,0:T(8,128)(2,1)S(1)}, bf16[1,2,4,320,128]{4,3,2,1,0:T(8,128)(2,1)S(1)}, u32[]{:S(2)}, u32[]{:S(2)}) collective-permute-start(bf16[1,2,4,320,128]{4,3,2,1,0:T(8,128)(2,1)S(1)} %copy-done), channel_id=1, source_target_pairs={{2,0},{3,1},{6,4},{7,5},{10,8},{11,9},{14,12},{15,13},{18,16},{19,... | collective-permute-start | bytes 1966088 | tf_op jit(solution)/shard_map/ppermute | solution.py:27
  23.2 1.0 copy-start.3
  47.4 43.5 %collective-permute-start.2 = (bf16[1,2,4,320,128]{4,3,2,1,0:T(8,128)(2,1)}, bf16[1,2,4,320,128]{4,3,2,1,0:T(8,128)(2,1)S(1)}, u32[]{:S(2)}, u32[]{:S(2)}) collective-permute-start(bf16[1,2,4,320,128]{4,3,2,1,0:T(8,128)(2,1)} %get-tuple-element.36), channel_id=1, source_target_pairs={{0,2},{1,3},{4,6},{5,7},{8,10},{9,11},{12,14},{13,15},{16,18},{17,... | collective-permute-start | bytes 1966088 | tf_op jit(solution)/shard_map/ppermute | solution.py:27
  50.3 9.1 %collective-permute-start.5 = (bf16[1,2,1,320,128]{4,3,2,1,0:T(8,128)(2,1)S(1)}, bf16[1,2,1,320,128]{4,3,2,1,0:T(8,128)(2,1)S(1)}, u32[]{:S(2)}, u32[]{:S(2)}) collective-permute-start(bf16[1,2,1,320,128]{4,3,2,1,0:T(8,128)(2,1)S(1)} %get-tuple-element.43), channel_id=1, source_target_pairs={{4,0},{8,4},{12,8},{5,1},{9,5},{13,9},{6,2},{10,6},{14,10},{7,3},{... | collective-permute-start | bytes 491528 | tf_op jit(solution)/shard_map/ppermute | solution.py:27
  51.6 7.7 %collective-permute-start.4 = (bf16[1,2,1,320,128]{4,3,2,1,0:T(8,128)(2,1)S(1)}, bf16[1,2,1,320,128]{4,3,2,1,0:T(8,128)(2,1)S(1)}, u32[]{:S(2)}, u32[]{:S(2)}) collective-permute-start(bf16[1,2,1,320,128]{4,3,2,1,0:T(8,128)(2,1)S(1)} %get-tuple-element.44), channel_id=1, source_target_pairs={{0,4},{4,8},{8,12},{1,5},{5,9},{9,13},{2,6},{6,10},{10,14},{3,7},{... | collective-permute-start | bytes 491528 | tf_op jit(solution)/shard_map/ppermute | solution.py:27
  57.5 2.0 %copy-start.1 = (bf16[1,2,4,320,128]{4,3,2,1,0:T(8,128)(2,1)S(1)}, bf16[1,2,4,320,128]{4,3,2,1,0:T(8,128)(2,1)}, u32[]{:S(2)}) copy-start(bf16[1,2,4,320,128]{4,3,2,1,0:T(8,128)(2,1)} %param.9) | copy-start | bytes 1966084
  57.5 2.0 %copy-start.6 = (f32[128]{0:T(128)S(1)}, f32[128]{0:T(128)}, u32[]{:S(2)}) copy-start(f32[128]{0:T(128)} %param.10) | copy-start | bytes 1540
  91.9 0.8 copy-start.2
  183.2 2.0 %copy-start.5 = (f32[3,128,128]{2,1,0:T(8,128)S(1)}, f32[3,128,128]{2,1,0:T(8,128)}, u32[]{:S(2)}) copy-start(f32[3,128,128]{2,1,0:T(8,128)} %get-tuple-element.32) | copy-start | bytes 589828
Sparse Core Ops, SparseCore 0:
  93.6 89.5 all-reduce.4
where the time goes:
time: 193 us
  waiting for transfers between devices  100 us (52%)
  blocking collectives  30 us (16%)
  matrix products  16.1 us (8%)
  starting transfers between devices  15.3 us (8%)
  between operations  14.4 us (7%)
  other arithmetic  13.6 us (7%)
  local copies, waits for them, and re-layouts  3.27 us (2%)
    psum x1, waiting for transfers between devices, shards(): lax.psum((grad_spatial, grad_temporal, grad_gain), ('rows', 'tm', 'dp'))  85.9 us
    psum x1, blocking collectives, shards(): lax.psum((grad_spatial, grad_temporal, grad_gain), ('rows', 'tm', 'dp'))  30 us
    dot_general x24, matrix products, product(): return jnp.dot(flatten(left), right, preferred_element_type=jnp.float32)  11.6 us
    ppermute x4, waiting for transfers between devices, passed_along(): return lax.ppermute(shard, axis, pairs)  9.45 us
    ppermute x4, starting transfers between devices, passed_along(): return lax.ppermute(shard, axis, pairs)  8.98 us
    ppermute x1, starting transfers between devices, extended(): before = lax.ppermute(last, axis, up)  4.94 us
    dot_general x12, matrix products, outer_sum(): lax.dot_general(flatten(left), flatten(right), (((0,), (0,)), ((), ())),...  4.54 us
    ppermute x1, waiting for transfers between devices, extended(): after = lax.ppermute(first, axis, down)  4.12 us
  transfers between devices with their start and end apart: 7, of which 5 were waited for; matrix products, arithmetic and copies ran while one was open for 6% of the time, Pallas kernels for 0%

commit v1 on v0

v1 whole, which is shorter than its diff:
```python
import functools
import math

import jax
import jax.numpy as jnp
from jax import lax
from jax.experimental import pallas as pl
from jax.experimental.pallas import tpu as pltpu
from jax.sharding import PartitionSpec as P

EPS = 1e-06
MESH = pl.DeviceIdType.MESH
F32 = jnp.float32
BF16 = jnp.bfloat16


def dot(a, b):
    return lax.dot_general(a, b, (((1,), (0,)), ((), ())), preferred_element_type=F32)


def dot_nt(a, b):
    return lax.dot_general(a, b, (((1,), (1,)), ((), ())), preferred_element_type=F32)


def kernel(
    sizes,
    scale,
    u_ref,
    gain_ref,
    ws_ref,
    wt_ref,
    cot_ref,
    out_ref,
    gin_ref,
    gs_ref,
    gt_ref,
    gg_ref,
    wsr,
    wtr,
    xs,
    xst,
    hid,
    act,
    actt,
    d3,
    nsend,
    nrecv,
    dsend,
    drecv,
    cotn,
    actp,
    g32,
    g16,
    rdp,
    s16,
    rbuf,
    r16,
    nss,
    nrs,
    dss,
    drs,
    css,
    crs,
    ass,
    ars,
    e1,
    rss,
    rrs,
    gss,
    grs,
    fss,
    frs,
):
    rows, tms, n, ch = sizes
    F, H, W, C = u_ref.shape
    C3 = 3 * C
    half = n * ch
    z = lax.axis_index("rows")
    t = lax.axis_index("tm")
    d = lax.axis_index("dp")
    p = t * rows + z

    def peer(o):
        q = lax.rem(p + o, n)
        return q, {"tm": q // rows, "rows": lax.rem(q, rows)}

    barrier = pltpu.get_barrier_semaphore()
    for o in range(1, n):
        pl.semaphore_signal(barrier, inc=1, device_id=peer(o)[1], device_id_type=MESH)
    partner = {"dp": 1 - d}
    pl.semaphore_signal(barrier, inc=1, device_id=partner, device_id_type=MESH)
    pl.semaphore_wait(barrier, n)

    def rcopy(src, dst, ss, rs, dev):
        return pltpu.make_async_remote_copy(
            src_ref=src, dst_ref=dst, send_sem=ss, recv_sem=rs, device_id=dev, device_id_type=MESH
        )

    order = [0, H - 1] + list(range(1, H - 1))
    inner = list(range(1, H - 1)) + [0, H - 1]

    def cot_copy(h):
        return rcopy(cot_ref.at[:, h], cotn.at[:, h], css.at[h], crs.at[h], {"tm": t - 1})

    def act_copy(h):
        return rcopy(act.at[:, h], actp.at[:, h], ass.at[h], ars.at[h], {"tm": t + 1})

    def n_copy(s):
        return rcopy(nsend.at[s], nrecv.at[s], nss.at[s], nrs.at[s], {"rows": z - 1 + 2 * s})

    def d_copy(s):
        return rcopy(dsend.at[s], drecv.at[s], dss.at[s], drs.at[s], {"rows": z - 1 + 2 * s})

    def has(s):
        return z > 0 if s == 0 else z < rows - 1

    @pl.when(t > 0)
    def _():
        for h in order:
            cot_copy(h).start()

    sub = lax.broadcasted_iota(jnp.int32, (W, C), 0)

    def shifted(x):
        before = jnp.where(sub == 0, 0.0, pltpu.roll(x, 1, 0))
        after = jnp.where(sub == W - 1, 0.0, pltpu.roll(x, W - 1, 0))
        return before, after

    def put_x(f, slot, x):
        before, after = shifted(x)
        for j, part in enumerate((before, x, after)):
            xs[f, slot, :, j * C : (j + 1) * C] = part.astype(BF16)
            xst[f, slot, j * C : (j + 1) * C, :] = part.T.astype(BF16)

    def put_d(f, slot, x):
        before, after = shifted(x)
        for j, part in enumerate((after, x, before)):
            d3[f, slot, :, j * C : (j + 1) * C] = part.astype(BF16)

    gain = gain_ref[...]

    def norm(f, h):
        u = u_ref[f, h].astype(F32)
        r = lax.rsqrt(jnp.mean(u * u, axis=-1, keepdims=True) + EPS)
        return r, u * r

    def each_frame(fn):
        def body(f, carry):
            fn(f)
            return carry

        lax.fori_loop(0, F, body, 0)

    for h in order:

        def fn(f, h=h):
            x = (norm(f, h)[1] * gain).astype(BF16)
            if h == 0:
                nsend[0, f] = x
            if h == H - 1:
                nsend[1, f] = x
            put_x(f, h + 1, x.astype(F32))

        each_frame(fn)
        if h == 0:

            @pl.when(has(0))
            def _():
                n_copy(0).start()

        if h == H - 1:

            @pl.when(has(1))
            def _():
                n_copy(1).start()

    for i in range(3):
        for j in range(3):
            wsr[i, :, j * C : (j + 1) * C] = ws_ref[i, j * C : (j + 1) * C, :]
    for k in range(3):
        wtr[:, k * C : (k + 1) * C] = wt_ref[k * C : (k + 1) * C, :]

    def halo(s, copy, recv, put):
        slot = H + 1 if s == 0 else 0

        @pl.when(has(1 - s))
        def _():
            copy(s).wait_recv()
            each_frame(lambda f: put(f, slot, recv[s, f].astype(F32)))

        @pl.when(jnp.logical_not(has(1 - s)))
        def _():
            each_frame(lambda f: put(f, slot, jnp.zeros((W, C), F32)))

    for h in inner:
        if h == 0:
            halo(1, n_copy, nrecv, put_x)
        if h == H - 1:
            halo(0, n_copy, nrecv, put_x)

        def fn(f, h=h):
            v = dot(xs[f, h], ws_ref[0]) + dot(xs[f, h + 1], ws_ref[1]) + dot(xs[f, h + 2], ws_ref[2])
            hid[f, h] = v
            a = v * jax.nn.sigmoid(v)
            act[f, h] = a.astype(BF16)
            actt[f, h] = a.T.astype(BF16)

        each_frame(fn)

        @pl.when(t < tms - 1)
        def _():
            act_copy(h).start()

    @pl.when(t == tms - 1)
    def _():
        cotn[...] = jnp.zeros_like(cotn)

    g32[...] = jnp.zeros_like(g32)
    for h in order:

        @pl.when(t < tms - 1)
        def _():
            cot_copy(h).wait_recv()

        cots = [cot_ref[f, h] for f in range(F)] + [cotn[f, h] for f in range(F)]
        tsum = None
        for f in range(F):
            cc = jnp.concatenate(cots[f : f + 3], axis=-1)
            dact = dot_nt(cc, wtr[...])
            v = hid[f, h]
            s = jax.nn.sigmoid(v)
            dh = (dact * s * (1.0 + v * (1.0 - s))).astype(BF16)
            if h == 0:
                dsend[0, f] = dh
            if h == H - 1:
                dsend[1, f] = dh
            put_d(f, h + 1, dh.astype(F32))
            term = dot(actt[f, h], cc)
            tsum = term if tsum is None else tsum + term
        if h == 0:

            @pl.when(has(0))
            def _():
                d_copy(0).start()

        if h == H - 1:

            @pl.when(has(1))
            def _():
                d_copy(1).start()

        for k in range(3):
            g32[3 * C3 + k * C : 3 * C3 + (k + 1) * C, :] += tsum[:, k * C : (k + 1) * C]
        for i in range(3):
            total = None
            for f in range(F):
                term = dot(xst[f, h + i], d3[f, h + 1, :, C : 2 * C])
                total = term if total is None else total + term
            g32[i * C3 : (i + 1) * C3, :] += total

    g16[...] = g32[...].astype(BF16)
    own = pl.multiple_of(d * half, 16)
    other = pl.multiple_of((1 - d) * half, 16)
    swap = rcopy(g16.at[pl.ds(other, half)], rdp, e1.at[0], e1.at[1], partner)
    swap.start()

    def back(f, h):
        dn = (
            dot_nt(d3[f, h + 2], wsr[0])
            + dot_nt(d3[f, h + 1], wsr[1])
            + dot_nt(d3[f, h], wsr[2])
        )
        r, unit = norm(f, h)
        du = dn * gain
        gin_ref[f, h] = (
            cot_ref[f, h].astype(F32)
            + r * (du - unit * jnp.mean(du * unit, axis=-1, keepdims=True))
        ).astype(BF16)

    swap.wait()
    g32[pl.ds(own, half), :] = g32[pl.ds(own, half), :] + rdp[...].astype(F32)
    s16[...] = g32[pl.ds(own, half), :].astype(BF16)

    def scatter(o):
        q, dev = peer(o)
        return rcopy(
            s16.at[pl.ds(pl.multiple_of(q * ch, 16), ch)],
            rbuf.at[o - 1],
            rss.at[o - 1],
            rrs.at[o - 1],
            dev,
        )

    for o in range(1, n):
        scatter(o).start()

    for h in range(1, H - 1):
        each_frame(functools.partial(back, h=h))

    total = g32[pl.ds(pl.multiple_of(own + p * ch, 8), ch), :]
    for o in range(1, n):
        scatter(o).wait_recv()
        total = total + rbuf[o - 1].astype(F32)

    def place(dd, q):
        return pl.ds(pl.multiple_of((dd * n + q) * ch, 16), ch)

    r16[place(d, p), :] = total.astype(BF16)

    def gather(o):
        return rcopy(r16.at[place(d, p)], r16.at[place(d, p)], gss.at[o - 1], grs.at[o - 1], peer(o)[1])

    def forward(o):
        ref = r16.at[place(d, lax.rem(p - o + n, n))]
        return rcopy(ref, ref, fss.at[o], frs.at[o], partner)

    for o in range(1, n):
        gather(o).start()
    forward(0).start()

    halo(1, d_copy, drecv, put_d)
    each_frame(functools.partial(back, h=0))
    halo(0, d_copy, drecv, put_d)
    each_frame(functools.partial(back, h=H - 1))

    @pl.when(t == 0)
    def _():
        actp[...] = jnp.zeros_like(actp)

    for o in range(1, n):
        gather(o).wait_recv()
        forward(o).start()

    for h in inner:

        @pl.when(t > 0)
        def _():
            act_copy(h).wait_recv()

        acts = [actp[f, h] for f in range(F)] + [act[f, h] for f in range(F)]
        for f in range(F):
            cc = jnp.concatenate([acts[F + f], acts[F + f - 1], acts[F + f - 2]], axis=-1)
            out_ref[f, h] = (u_ref[f, h].astype(F32) + dot(cc, wt_ref[...])).astype(BF16)

    for o in range(n):
        forward(o).wait_recv()
    total = None
    for b in range(9):
        g = r16[b * C : (b + 1) * C, :].astype(F32) * scale
        gs_ref[b] = g
        term = g * ws_ref[b // 3, (b % 3) * C : (b % 3 + 1) * C, :].astype(F32)
        total = term if total is None else total + term
    gg_ref[...] = jnp.sum(total.T, axis=0, keepdims=True) / gain
    for k in range(3):
        gt_ref[k] = r16[(9 + k) * C : (10 + k) * C, :].astype(F32) * scale

    for o in range(1, n):
        scatter(o).wait_send()
        gather(o).wait_send()
    for o in range(n):
        forward(o).wait_send()
    for s in range(2):

        @pl.when(has(s))
        def _():
            n_copy(s).wait_send()
            d_copy(s).wait_send()

    @pl.when(t > 0)
    def _():
        for h in range(H):
            cot_copy(h).wait_send()

    @pl.when(t < tms - 1)
    def _():
        for h in range(H):
            act_copy(h).wait_send()


def shards(frames_in, gain, spatial_w, temporal_w, cotangent):
    _, F, H, W, C = frames_in.shape
    rows, tms, dps = lax.axis_size("rows"), lax.axis_size("tm"), lax.axis_size("dp")
    n = rows * tms
    ch = -(-12 * C // (dps * n * 16)) * 16
    total = dps * n * ch
    scale = 1.0 / math.sqrt(F * H * W * n * dps)
    shape = (F, H, W, C)
    vmem = pl.BlockSpec(memory_space=pltpu.VMEM)
    dma = pltpu.SemaphoreType.DMA
    out = pl.pallas_call(
        functools.partial(kernel, (rows, tms, n, ch), scale),
        out_shape=(
            jax.ShapeDtypeStruct(shape, BF16),
            jax.ShapeDtypeStruct(shape, BF16),
            jax.ShapeDtypeStruct((9, C, C), F32),
            jax.ShapeDtypeStruct((3, C, C), F32),
            jax.ShapeDtypeStruct((1, C), F32),
        ),
        in_specs=[vmem] * 5,
        out_specs=(vmem,) * 5,
        scratch_shapes=[
            pltpu.VMEM((3, C, 3 * C), BF16),
            pltpu.VMEM((C, 3 * C), BF16),
            pltpu.VMEM((F, H + 2, W, 3 * C), BF16),
            pltpu.VMEM((F, H + 2, 3 * C, W), BF16),
            pltpu.VMEM(shape, F32),
            pltpu.VMEM(shape, BF16),
            pltpu.VMEM((F, H, C, W), BF16),
            pltpu.VMEM((F, H + 2, W, 3 * C), BF16),
            pltpu.VMEM((2, F, W, C), BF16),
            pltpu.VMEM((2, F, W, C), BF16),
            pltpu.VMEM((2, F, W, C), BF16),
            pltpu.VMEM((2, F, W, C), BF16),
            pltpu.VMEM(shape, BF16),
            pltpu.VMEM(shape, BF16),
            pltpu.VMEM((total, C), F32),
            pltpu.VMEM((total, C), BF16),
            pltpu.VMEM((n * ch, C), BF16),
            pltpu.VMEM((n * ch, C), BF16),
            pltpu.VMEM((n - 1, ch, C), BF16),
            pltpu.VMEM((total, C), BF16),
            dma((2,)),
            dma((2,)),
            dma((2,)),
            dma((2,)),
            dma((H,)),
            dma((H,)),
            dma((H,)),
            dma((H,)),
            dma((2,)),
            dma((n - 1,)),
            dma((n - 1,)),
            dma((n - 1,)),
            dma((n - 1,)),
            dma((n,)),
            dma((n,)),
        ],
        compiler_params=pltpu.CompilerParams(
            collective_id=0, has_side_effects=True, vmem_limit_bytes=48 * 1024 * 1024
        ),
    )(
        frames_in.reshape(shape),
        gain.reshape(1, C),
        spatial_w.reshape(3, 3 * C, C),
        temporal_w.reshape(3 * C, C),
        cotangent.reshape(shape),
    )
    block_out, grad_input, gs, gt, gg = out
    return (
        block_out.reshape(frames_in.shape),
        grad_input.reshape(frames_in.shape),
        gs.reshape(3, 3, C, C),
        gt,
        gg.reshape(C),
    )


def solution(mesh):
    split = P(("groups", "dp"), "tm", "rows", None, None)
    return jax.shard_map(
        shards,
        mesh=mesh,
        in_specs=(split, P(), P(), P(), split),
        out_specs=(split, split, P("groups", None, None, None), P("groups", None, None), P("groups")),
        check_vma=False,
    )
```

time: 193 us -> 46 us (0.24)
  waiting for transfers between devices: 100 us -> 0 us
  Pallas kernels: 0 us -> 36.7 us
  blocking collectives: 30 us -> 0 us
  matrix products: 16.1 us -> 0 us
  starting transfers between devices: 15.3 us -> 0 us
  between operations: 14.4 us -> 0.66 us
  other arithmetic: 13.6 us -> 0 us
  local copies, waits for them, and re-layouts: 3.27 us -> 8.35 us
    psum x1 -> x0, waiting for transfers between devices: 85.9 us -> none  [shards(): lax.psum((grad_spatial, grad_temporal, grad_gain), ('rows', 'tm', 'dp'))]
    pallas_call x0 -> x1, Pallas kernels: none -> 36.7 us  [shards(): pl.pallas_call(functools.partial(kernel, (rows, tms, n, ch), scale), out_...]
    psum x1 -> x0, blocking collectives: 30 us -> none  [shards(): lax.psum((grad_spatial, grad_temporal, grad_gain), ('rows', 'tm', 'dp'))]
    dot_general x36 -> x0, matrix products: 16.1 us -> none  [the longest x24 11.6 us: product(): return jnp.dot(flatten(left), right, preferred_element_type=jnp.float32)]
    ppermute x6 -> x0, starting transfers between devices: 15.2 us -> none  [the longest x4 8.98 us: passed_along(): return lax.ppermute(shard, axis, pairs)]
    ppermute x6 -> x0, waiting for transfers between devices: 14.1 us -> none  [the longest x4 9.45 us: passed_along(): return lax.ppermute(shard, axis, pairs)]
    unnamed x14 -> x15, local copies, waits for them, and re-layouts: 0.2 us -> 8.35 us
    convert_element_type x3 -> x0, other arithmetic: 4.6 us -> none  [the longest x1 1.63 us: shards(): grad_input = (cotangent.astype(jnp.float32) + recip * (dunit - unit * jnp...]
  transfers between devices with their start and end apart: 7 -> 0, of which waited for: 5 -> 0; matrix products, arithmetic and copies ran while one was open for 6% -> 0% of each run, Pallas kernels for 0% -> 0%
where the time goes in v1:
time: 46 us; the launch traced here: 45.7 us
  Pallas kernels  36.7 us (80%)
  local copies, waits for them, and re-layouts  8.35 us (18%)
  between operations  0.66 us (1%)
    pallas_call x1, Pallas kernels, shards(): pl.pallas_call(functools.partial(kernel, (rows, tms, n, ch), scale), out_...  36.7 us
    unnamed x15, local copies, waits for them, and re-layouts  8.35 us

profile of v1, /device:TPU:0, one launch (start us, length us, event | category | flops | bytes accessed | tf_op | source)
XLA Modules:
  0.0 45.7 jit_solution(16650674253763392375)
XLA Ops:
  0.6 0.0 copy-start.4
  0.6 0.6 %copy-done.4 = f32[128]{0:T(128)S(1)} copy-done((f32[128]{0:T(128)S(1)}, f32[128]{0:T(128)}, u32[]{:S(2)}) %copy-start.4) | copy-done | bytes 536
  1.3 0.0 copy-start
  1.3 1.1 %copy-done = bf16[1,2,4,320,128]{4,3,2,1,0:T(8,128)(2,1)S(1)} copy-done((bf16[1,2,4,320,128]{4,3,2,1,0:T(8,128)(2,1)S(1)}, bf16[1,2,4,320,128]{4,3,2,1,0:T(8,128)(2,1)}, u32[]{:S(2)}) %copy-start) | copy-done | bytes 655384
  2.4 0.0 copy-start.1
  2.4 1.1 %copy-done.1 = bf16[1,2,4,320,128]{4,3,2,1,0:T(8,128)(2,1)S(1)} copy-done((bf16[1,2,4,320,128]{4,3,2,1,0:T(8,128)(2,1)S(1)}, bf16[1,2,4,320,128]{4,3,2,1,0:T(8,128)(2,1)}, u32[]{:S(2)}) %copy-start.1) | copy-done | bytes 655384
  3.5 0.0 copy-start.2
  3.5 1.0 %copy-done.2 = bf16[3,3,128,128]{3,2,1,0:T(8,128)(2,1)S(1)} copy-done((bf16[3,3,128,128]{3,2,1,0:T(8,128)(2,1)S(1)}, bf16[3,3,128,128]{3,2,1,0:T(8,128)(2,1)}, u32[]{:S(2)}) %copy-start.2) | copy-done | bytes 294936
  4.4 0.0 copy-start.3
  4.4 0.9 %copy-done.3 = bf16[3,128,128]{2,1,0:T(8,128)(2,1)S(1)} copy-done((bf16[3,128,128]{2,1,0:T(8,128)(2,1)S(1)}, bf16[3,128,128]{2,1,0:T(8,128)(2,1)}, u32[]{:S(2)}) %copy-start.3) | copy-done | bytes 98328
  5.3 36.7 %shard_map.92 = (bf16[2,4,320,128]{3,2,1,0:T(8,128)(2,1)S(1)}, bf16[2,4,320,128]{3,2,1,0:T(8,128)(2,1)S(1)}, f32[9,128,128]{2,1,0:T(8,128)S(1)}, f32[3,128,128]{2,1,0:T(8,128)S(1)}, f32[1,128]{1,0:T(1,128)S(1)}) custom-call(bf16[2,4,320,128]{3,2,1,0:T(8,128)(2,1)S(1)} %bitcast.9, f32[1,128]{1,0:T(1,128)S(1)} %bitcast.16, bf16[3,384,128]{2,1,0:T(8,128)(2,1)S(1)} %bitcast.14, ...), custom_call_target="tpu_custom_call" | custom-call | tf_op jit(solution)/shard_map/pallas_call | solution.py:390
  42.0 0.8 %copy.15 = bf16[1,2,4,320,128]{4,3,2,1,0:T(8,128)(2,1)} copy(bf16[1,2,4,320,128]{4,3,2,1,0:T(8,128)(2,1)S(1)} %bitcast.12) | data formatting | bytes 1310720
  42.9 0.8 %copy.16 = bf16[1,2,4,320,128]{4,3,2,1,0:T(8,128)(2,1)} copy(bf16[1,2,4,320,128]{4,3,2,1,0:T(8,128)(2,1)S(1)} %bitcast.11) | data formatting | bytes 1310720
  43.7 0.8 %copy.17 = f32[3,3,128,128]{3,2,1,0:T(8,128)} copy(f32[3,3,128,128]{3,2,1,0:T(8,128)S(1)} %bitcast.13) | data formatting | bytes 1179648
  44.5 0.7 %copy.18 = f32[3,128,128]{2,1,0:T(8,128)} copy(f32[3,128,128]{2,1,0:T(8,128)S(1)} %get-tuple-element.23) | data formatting | bytes 393216
  45.2 0.5 %copy.19 = f32[128]{0:T(128)} copy(f32[128]{0:T(128)S(1)} %bitcast.17) | data formatting | bytes 1024
Async XLA Ops:
  0.6 0.7 %copy-start.4 = (f32[128]{0:T(128)S(1)}, f32[128]{0:T(128)}, u32[]{:S(2)}) copy-start(f32[128]{0:T(128)} %param.6) | copy-start | bytes 1540
  1.3 1.1 %copy-start = (bf16[1,2,4,320,128]{4,3,2,1,0:T(8,128)(2,1)S(1)}, bf16[1,2,4,320,128]{4,3,2,1,0:T(8,128)(2,1)}, u32[]{:S(2)}) copy-start(bf16[1,2,4,320,128]{4,3,2,1,0:T(8,128)(2,1)} %param.5) | copy-start | bytes 1966084
  2.4 1.1 %copy-start.1 = (bf16[1,2,4,320,128]{4,3,2,1,0:T(8,128)(2,1)S(1)}, bf16[1,2,4,320,128]{4,3,2,1,0:T(8,128)(2,1)}, u32[]{:S(2)}) copy-start(bf16[1,2,4,320,128]{4,3,2,1,0:T(8,128)(2,1)} %param.9) | copy-start | bytes 1966084
  3.5 1.0 %copy-start.2 = (bf16[3,3,128,128]{3,2,1,0:T(8,128)(2,1)S(1)}, bf16[3,3,128,128]{3,2,1,0:T(8,128)(2,1)}, u32[]{:S(2)}) copy-start(bf16[3,3,128,128]{3,2,1,0:T(8,128)(2,1)} %param.7) | copy-start | bytes 884740
  4.4 0.9 %copy-start.3 = (bf16[3,128,128]{2,1,0:T(8,128)(2,1)S(1)}, bf16[3,128,128]{2,1,0:T(8,128)(2,1)}, u32[]{:S(2)}) copy-start(bf16[3,128,128]{2,1,0:T(8,128)(2,1)} %param.8) | copy-start | bytes 294916

commit v2 on v1

--- a/solution.py
+++ b/solution.py
@@ -25,16 +25,24 @@
 def kernel(
     sizes,
     scale,
+    u_in,
+    gain_ref,
+    ws_in,
+    wt_in,
+    cot_in,
+    out_hbm,
+    gin_hbm,
+    gs_ref,
+    gt_ref,
+    gg_ref,
     u_ref,
-    gain_ref,
     ws_ref,
     wt_ref,
     cot_ref,
+    lsem,
     out_ref,
     gin_ref,
-    gs_ref,
-    gt_ref,
-    gg_ref,
+    osem,
     wsr,
     wtr,
     xs,
@@ -73,6 +81,14 @@
 ):
     rows, tms, n, ch = sizes
     F, H, W, C = u_ref.shape
+    loads = [
+        pltpu.make_async_copy(a, b, lsem.at[i])
+        for i, (a, b) in enumerate(
+            ((u_in, u_ref), (ws_in, ws_ref), (cot_in, cot_ref), (wt_in, wt_ref))
+        )
+    ]
+    for load in loads:
+        load.start()
     C3 = 3 * C
     half = n * ch
     z = lax.axis_index("rows")
@@ -100,7 +116,7 @@
     inner = list(range(1, H - 1)) + [0, H - 1]
 
     def cot_copy(h):
-        return rcopy(cot_ref.at[:, h], cotn.at[:, h], css.at[h], crs.at[h], {"tm": t - 1})
+        return rcopy(cot_in.at[:, h], cotn.at[:, h], css.at[h], crs.at[h], {"tm": t - 1})
 
     def act_copy(h):
         return rcopy(act.at[:, h], actp.at[:, h], ass.at[h], ars.at[h], {"tm": t + 1})
@@ -138,6 +154,7 @@
             d3[f, slot, :, j * C : (j + 1) * C] = part.astype(BF16)
 
     gain = gain_ref[...]
+    loads[0].wait()
 
     def norm(f, h):
         u = u_ref[f, h].astype(F32)
@@ -174,6 +191,8 @@
             def _():
                 n_copy(1).start()
 
+    for load in loads[1:]:
+        load.wait()
     for i in range(3):
         for j in range(3):
             wsr[i, :, j * C : (j + 1) * C] = ws_ref[i, j * C : (j + 1) * C, :]
@@ -214,6 +233,21 @@
     @pl.when(t == tms - 1)
     def _():
         cotn[...] = jnp.zeros_like(cotn)
+
+    def mix(late):
+        for h in inner:
+            if late:
+                act_copy(h).wait_recv()
+            acts = [actp[f, h] if late else None for f in range(F)] + [act[f, h] for f in range(F)]
+            for f in range(F):
+                parts = [a for a in (acts[F + f], acts[F + f - 1], acts[F + f - 2]) if a is not None]
+                cc = jnp.concatenate(parts, axis=-1)
+                mixed = dot(cc, wt_ref[: len(parts) * C, :])
+                out_ref[f, h] = (u_ref[f, h].astype(F32) + mixed).astype(BF16)
+
+    @pl.when(t == 0)
+    def _():
+        mix(False)
 
     g32[...] = jnp.zeros_like(g32)
     for h in order:
@@ -323,24 +357,20 @@
     halo(0, d_copy, drecv, put_d)
     each_frame(functools.partial(back, h=H - 1))
 
-    @pl.when(t == 0)
-    def _():
-        actp[...] = jnp.zeros_like(actp)
-
     for o in range(1, n):
         gather(o).wait_recv()
         forward(o).start()
 
-    for h in inner:
-
-        @pl.when(t > 0)
-        def _():
-            act_copy(h).wait_recv()
-
-        acts = [actp[f, h] for f in range(F)] + [act[f, h] for f in range(F)]
-        for f in range(F):
-            cc = jnp.concatenate([acts[F + f], acts[F + f - 1], acts[F + f - 2]], axis=-1)
-            out_ref[f, h] = (u_ref[f, h].astype(F32) + dot(cc, wt_ref[...])).astype(BF16)
+    @pl.when(t > 0)
+    def _():
+        mix(True)
+
+    stores = [
+        pltpu.make_async_copy(gin_ref, gin_hbm, osem.at[0]),
+        pltpu.make_async_copy(out_ref, out_hbm, osem.at[1]),
+    ]
+    for store in stores:
+        store.start()
 
     for o in range(n):
         forward(o).wait_recv()
@@ -354,6 +384,8 @@
     for k in range(3):
         gt_ref[k] = r16[(9 + k) * C : (10 + k) * C, :].astype(F32) * scale
 
+    for store in stores:
+        store.wait()
     for o in range(1, n):
         scatter(o).wait_send()
         gather(o).wait_send()
@@ -375,6 +407,18 @@
     def _():
         for h in range(H):
             act_copy(h).wait_send()
+
+
+def settle(*refs):
+    count = len(refs) // 2
+    sems = refs[-1]
+    copies = [
+        pltpu.make_async_copy(refs[i], refs[count + i], sems.at[i]) for i in range(count)
+    ]
+    for copy in copies:
+        copy.start()
+    for copy in copies:
+        copy.wait()
 
 
 def shards(frames_in, gain, spatial_w, temporal_w, cotangent):
@@ -386,6 +430,7 @@
     scale = 1.0 / math.sqrt(F * H * W * n * dps)
     shape = (F, H, W, C)
     vmem = pl.BlockSpec(memory_space=pltpu.VMEM)
+    hbm = pl.BlockSpec(memory_space=pl.ANY)
     dma = pltpu.SemaphoreType.DMA
     out = pl.pallas_call(
         functools.partial(kernel, (rows, tms, n, ch), scale),
@@ -396,9 +441,17 @@
             jax.ShapeDtypeStruct((3, C, C), F32),
             jax.ShapeDtypeStruct((1, C), F32),
         ),
-        in_specs=[vmem] * 5,
-        out_specs=(vmem,) * 5,
+        in_specs=[hbm, vmem, hbm, hbm, hbm],
+        out_specs=(hbm, hbm, vmem, vmem, vmem),
         scratch_shapes=[
+            pltpu.VMEM(shape, BF16),
+            pltpu.VMEM((3, 3 * C, C), BF16),
+            pltpu.VMEM((3 * C, C), BF16),
+            pltpu.VMEM(shape, BF16),
+            dma((4,)),
+            pltpu.VMEM(shape, BF16),
+            pltpu.VMEM(shape, BF16),
+            dma((2,)),
             pltpu.VMEM((3, C, 3 * C), BF16),
             pltpu.VMEM((C, 3 * C), BF16),
             pltpu.VMEM((F, H + 2, W, 3 * C), BF16),
@@ -436,7 +489,7 @@
             dma((n,)),
         ],
         compiler_params=pltpu.CompilerParams(
-            collective_id=0, has_side_effects=True, vmem_limit_bytes=48 * 1024 * 1024
+            collective_id=0, has_side_effects=True, vmem_limit_bytes=63 * 1024 * 1024
         ),
     )(
         frames_in.reshape(shape),
@@ -445,7 +498,14 @@
         temporal_w.reshape(3 * C, C),
         cotangent.reshape(shape),
     )
-    block_out, grad_input, gs, gt, gg = out
+    anywhere = pl.BlockSpec(memory_space=pl.ANY)
+    block_out, grad_input, gs, gt, gg = pl.pallas_call(
+        settle,
+        out_shape=tuple(jax.ShapeDtypeStruct(o.shape, o.dtype) for o in out),
+        in_specs=[vmem] * len(out),
+        out_specs=(anywhere,) * len(out),
+        scratch_shapes=[dma((len(out),))],
+    )(*out)
     return (
         block_out.reshape(frames_in.shape),
         grad_input.reshape(frames_in.shape),

time: 46 us -> 42 us (0.913)
  local copies, waits for them, and re-layouts: 8.35 us -> 0 us
  Pallas kernels: 36.7 us -> 41.1 us
    unnamed x15 -> x0, local copies, waits for them, and re-layouts: 8.35 us -> none
    pallas_call x0 -> x1, Pallas kernels: none -> 2.87 us  [shards(): pl.pallas_call(settle, out_shape=tuple((jax.ShapeDtypeStruct(o.shape, o.d...]
    pallas_call x1, Pallas kernels: 36.7 us -> 38.3 us  [shards(): pl.pallas_call(functools.partial(kernel, (rows, tms, n, ch), scale), out_...]
where the time goes in v2:
time: 42 us; the launch traced here: 41.8 us
  Pallas kernels  41.1 us (98%)
  between operations  0.64 us (2%)
    pallas_call x1, Pallas kernels, shards(): pl.pallas_call(functools.partial(kernel, (rows, tms, n, ch), scale), out_...  38.3 us
    pallas_call x1, Pallas kernels, shards(): pl.pallas_call(settle, out_shape=tuple((jax.ShapeDtypeStruct(o.shape, o.d...  2.87 us

profile of v2, /device:TPU:0, one launch (start us, length us, event | category | flops | bytes accessed | tf_op | source)
XLA Modules:
  0.0 41.8 jit_solution(8045933387487658839)
XLA Ops:
  0.6 38.3 %shard_map.92 = (bf16[2,4,320,128]{3,2,1,0:T(8,128)(2,1)}, bf16[2,4,320,128]{3,2,1,0:T(8,128)(2,1)}, f32[9,128,128]{2,1,0:T(8,128)}, f32[3,128,128]{2,1,0:T(8,128)}, f32[1,128]{1,0:T(1,128)}) custom-call(bf16[2,4,320,128]{3,2,1,0:T(8,128)(2,1)} %bitcast.9, f32[1,128]{1,0:T(1,128)} %bitcast.13, bf16[3,384,128]{2,1,0:T(8,128)(2,1)} %bitcast.11, ...), custom_call_target="tpu_custom_call" | custom-call | tf_op jit(solution)/shard_map/pallas_call | solution.py:435
  38.9 2.9 %shard_map.93 = (bf16[2,4,320,128]{3,2,1,0:T(8,128)(2,1)}, bf16[2,4,320,128]{3,2,1,0:T(8,128)(2,1)}, f32[9,128,128]{2,1,0:T(8,128)}, f32[3,128,128]{2,1,0:T(8,128)}, f32[1,128]{1,0:T(1,128)}) custom-call(bf16[2,4,320,128]{3,2,1,0:T(8,128)(2,1)} %get-tuple-element.15.refs_0_, bf16[2,4,320,128]{3,2,1,0:T(8,128)(2,1)} %get-tuple-element.16.refs_1_, ...), custom_call_target="tpu_custom_call" | custom-call | tf_op jit(solution)/shard_map/pallas_call | solution.py:502

commit v3 on v2

--- a/solution.py
+++ b/solution.py
@@ -311,6 +311,7 @@
             + r * (du - unit * jnp.mean(du * unit, axis=-1, keepdims=True))
         ).astype(BF16)
 
+    each_frame(functools.partial(back, h=1))
     swap.wait()
     g32[pl.ds(own, half), :] = g32[pl.ds(own, half), :] + rdp[...].astype(F32)
     s16[...] = g32[pl.ds(own, half), :].astype(BF16)
@@ -328,7 +329,7 @@
     for o in range(1, n):
         scatter(o).start()
 
-    for h in range(1, H - 1):
+    for h in range(2, H - 1):
         each_frame(functools.partial(back, h=h))
 
     total = g32[pl.ds(pl.multiple_of(own + p * ch, 8), ch), :]

time: 42 us -> 42 us (level)
  no operation moved by 1% of the time
where the time goes in v3:
time: 42 us; the launch traced here: 41.8 us
  Pallas kernels  41.1 us (98%)
  between operations  0.64 us (2%)
    pallas_call x1, Pallas kernels, shards(): pl.pallas_call(functools.partial(kernel, (rows, tms, n, ch), scale), out_...  38.3 us
    pallas_call x1, Pallas kernels, shards(): pl.pallas_call(settle, out_shape=tuple((jax.ShapeDtypeStruct(o.shape, o.d...  2.87 us

profile of v3, /device:TPU:0, one launch (start us, length us, event | category | flops | bytes accessed | tf_op | source)
XLA Modules:
  0.0 41.8 jit_solution(6839051201625939665)
XLA Ops:
  0.6 38.3 %shard_map.92 = (bf16[2,4,320,128]{3,2,1,0:T(8,128)(2,1)}, bf16[2,4,320,128]{3,2,1,0:T(8,128)(2,1)}, f32[9,128,128]{2,1,0:T(8,128)}, f32[3,128,128]{2,1,0:T(8,128)}, f32[1,128]{1,0:T(1,128)}) custom-call(bf16[2,4,320,128]{3,2,1,0:T(8,128)(2,1)} %bitcast.9, f32[1,128]{1,0:T(1,128)} %bitcast.13, bf16[3,384,128]{2,1,0:T(8,128)(2,1)} %bitcast.11, ...), custom_call_target="tpu_custom_call" | custom-call | tf_op jit(solution)/shard_map/pallas_call | solution.py:436
  38.9 2.9 %shard_map.93 = (bf16[2,4,320,128]{3,2,1,0:T(8,128)(2,1)}, bf16[2,4,320,128]{3,2,1,0:T(8,128)(2,1)}, f32[9,128,128]{2,1,0:T(8,128)}, f32[3,128,128]{2,1,0:T(8,128)}, f32[1,128]{1,0:T(1,128)}) custom-call(bf16[2,4,320,128]{3,2,1,0:T(8,128)(2,1)} %get-tuple-element.15.refs_0_, bf16[2,4,320,128]{3,2,1,0:T(8,128)(2,1)} %get-tuple-element.16.refs_1_, ...), custom_call_target="tpu_custom_call" | custom-call | tf_op jit(solution)/shard_map/pallas_call | solution.py:503
